TPU v7x, 32 devices: a whole 2x2x4 slice. The times are simulated.
32 devices in a mesh: neuron: 8 (over z, y), tm: 4 (over x, core).
Axes of the slice: x: 2, y: 2, z: 4, core: 2. Of those that a mesh axis runs over, the one named last changes fastest.
Arguments:
- data: bfloat16 [1024, 8192], P('neuron', 'tm'), may hold values from 0 to 2
- behaviour: bfloat16 [512, 8192], P('neuron', 'tm'), may hold values from 0 to 2
- motifs: bfloat16 [32, 1024, 128], P('tm', 'neuron'), may hold values from 0 to 2
- behav_motifs: bfloat16 [32, 512, 128], P('tm', 'neuron'), may hold values from 0 to 2
- activations: bfloat16 [128, 8192], P(None, 'tm'), may hold values from 0 to 2
Outputs:
- new_motifs: bfloat16 [32, 1024, 128], P('tm', 'neuron')
- new_behav_motifs: bfloat16 [32, 512, 128], P('tm', 'neuron')
- new_activations: bfloat16 [128, 8192], P(None, 'tm')
All inputs are finite; a program needn't handle non-finite values.
Results may differ from a plain program's by a relative error of at most 0.0034.
Values may be sent and summed in bfloat16 or wider, within the bound.
A program may use at most 64 MiB of HBM per device.

v0:
```python
import math

import jax
import jax.numpy as jnp
from jax import lax
from jax.sharding import PartitionSpec as P

behaviour_weight = 2.0


def passed_along(shard, axis, by):
    peers = lax.axis_size(axis)
    pairs = [(i, i + by) for i in range(peers) if 0 <= i + by < peers]
    return lax.ppermute(shard, axis, pairs)


def local(data, behaviour, motifs, behav_motifs, activations):
    lags_here, neurons_here, width = motifs.shape
    features_here = behaviour.shape[0]
    frames = activations.shape[1]
    lag_count = lags_here * lax.axis_size("tm")
    all_frames = frames * lax.axis_size("tm")
    all_neurons = neurons_here * lax.axis_size("neuron")
    all_features = features_here * lax.axis_size("neuron")
    scale = 1.0 / (lag_count * width)
    rate_motif = 0.5 * lag_count * width / math.sqrt(all_frames)
    rate_active = 0.5 * lag_count * width / math.sqrt(lag_count * (all_neurons + 4 * all_features))
    rim = lag_count - 1
    earlier = passed_along(activations[:, frames - rim :], "tm", 1)
    extended = jnp.concatenate([earlier, activations], axis=1)

    def window(lag):
        return lax.dynamic_slice_in_dim(extended, rim - lag, frames, 1)

    zero_pair = (
        jnp.zeros((neurons_here, frames), jnp.float32),
        jnp.zeros((features_here, frames), jnp.float32),
    )
    back_start = jnp.zeros((width, rim + frames), jnp.float32)
    gathered = (
        lax.all_gather(motifs, "tm", axis=0, tiled=True),
        lax.all_gather(behav_motifs, "tm", axis=0, tiled=True),
    )

    def one_lag(index, acc):
        win = window(0 + index)
        neuron_rows = lax.dynamic_index_in_dim(gathered[0], index, 0, keepdims=False)
        feature_rows = lax.dynamic_index_in_dim(gathered[1], index, 0, keepdims=False)
        return (
            acc[0] + jnp.dot(neuron_rows, win, preferred_element_type=jnp.float32),
            acc[1] + jnp.dot(feature_rows, win, preferred_element_type=jnp.float32),
        )

    recon_x, recon_b = lax.fori_loop(0, gathered[0].shape[0], one_lag, zero_pair)
    resid_x = (data.astype(jnp.float32) - scale * recon_x).astype(jnp.bfloat16)
    resid_b = (behaviour_weight * (behaviour.astype(jnp.float32) - scale * recon_b)).astype(
        jnp.bfloat16
    )

    def one_lag(index, acc):
        lag = 0 + index
        neuron_rows = lax.dynamic_index_in_dim(gathered[0], index, 0, keepdims=False)
        feature_rows = lax.dynamic_index_in_dim(gathered[1], index, 0, keepdims=False)
        back = lax.dot_general(
            neuron_rows, resid_x, (((0,), (0,)), ((), ())), preferred_element_type=jnp.float32
        )
        back = back + lax.dot_general(
            feature_rows, resid_b, (((0,), (0,)), ((), ())), preferred_element_type=jnp.float32
        )
        place = rim - lag
        current = lax.dynamic_slice_in_dim(acc, place, frames, 1)
        return lax.dynamic_update_slice_in_dim(acc, current + back, place, 1)

    extended_back = lax.fori_loop(0, gathered[0].shape[0], one_lag, back_start)

    def one_lag(index):
        win = window(index)
        neuron_part = lax.dot_general(
            resid_x, win, (((1,), (1,)), ((), ())), preferred_element_type=jnp.float32
        )
        feature_part = lax.dot_general(
            resid_b, win, (((1,), (1,)), ((), ())), preferred_element_type=jnp.float32
        )
        return -scale * jnp.concatenate([neuron_part, feature_part], axis=0)

    gradients = lax.psum_scatter(
        lax.map(one_lag, jnp.arange(lags_here * lax.axis_size("tm"), dtype=jnp.int32)),
        "tm",
        scatter_dimension=0,
        tiled=True,
    )
    grad_motif = gradients[:, :neurons_here]
    grad_behav = gradients[:, neurons_here:]
    new_motifs = jnp.maximum(motifs.astype(jnp.float32) - rate_motif * grad_motif, 0.0).astype(
        jnp.bfloat16
    )
    new_behav = jnp.maximum(behav_motifs.astype(jnp.float32) - rate_motif * grad_behav, 0.0).astype(
        jnp.bfloat16
    )
    spilled = extended_back[:, :rim]
    from_next = passed_along(spilled, "tm", -1)
    own_part = extended_back[:, rim:]
    own_part = own_part.at[:, frames - rim :].add(from_next)
    partial_grad = -scale * own_part
    grad_active = lax.psum(partial_grad, "neuron")
    new_active = jnp.maximum(
        activations.astype(jnp.float32) - rate_active * grad_active, 0.0
    ).astype(jnp.bfloat16)
    return (new_motifs, new_behav, new_active)


def solution(mesh):
    placed = (
        P("neuron", "tm"),
        P("neuron", "tm"),
        P("tm", "neuron", None),
        P("tm", "neuron", None),
        P(None, "tm"),
    )
    return jax.shard_map(
        local,
        mesh=mesh,
        in_specs=placed,
        out_specs=(P("tm", "neuron", None), P("tm", "neuron", None), P(None, "tm")),
        check_vma=False,
    )
```

profile of v0, /device:TPU:0, one launch (start us, length us, event | category | flops | bytes accessed | tf_op | source)
XLA Modules:
  0.0 433.7 jit_solution(9646711238752981994)
XLA Ops:
  11.2 10.2 %all_gather.7 = bf16[32,64,128]{2,1,0:T(8,128)(2,1)} all-gather(bf16[8,64,128]{2,1,0:T(8,128)(2,1)} %param.16), channel_id=1, replica_groups=mesh['neuron'=8,'tm'=4] {'tm'}, dimensions={0}, use_global_device_ids=true | all-gather | bytes 655360 | tf_op jit(solution)/shard_map/all_gather | solution.py:42
  21.6 7.4 %all-gather.2.cloned.1.call-done = bf16[32,128,128]{2,1,0:T(8,128)(2,1)} async-done(((bf16[8,128,128]{2,1,0:T(8,128)(2,1)}), bf16[32,128,128]{2,1,0:T(8,128)(2,1)}) %all-gather.2.cloned.1.call-update) | async-done | bytes 1048592 | tf_op jit(solution)/shard_map/all_gather | solution.py:41
  29.0 80.4 %while.48 = (s32[]{:T(128)}, f32[128,2048]{1,0:T(8,128)S(1)}, f32[64,2048]{1,0:T(8,128)S(1)}, bf16[32,128,128]{2,1,0:T(8,128)(2,1)}, bf16[128,2079]{1,0:T(8,128)...) while((s32[]{:T(128)}, f32[128,2048]{1,0:T(8,128)S(1)}, ...), condition=%wide.region_1.2_spmd.clone, body=%wide.region_0.1_spmd.clone.sunk | while | flops 101449736 | bytes 4244646 | solution.py:54
  110.6 157.4 %while.47 = (s32[]{:T(128)}, f32[128,2079]{1,0:T(8,128)S(1)}, bf16[32,128,128]{2,1,0:T(8,128)(2,1)}, bf16[128,2048]{1,0:T(8,128)(2,1)S(1)}, bf16[32,64,128]{2,1,...) while((s32[]{:T(128)}, f32[128,2079]{1,0:T(8,128)S(1)}, ...), condition=%wide.region_6.7_spmd, body=%wide.region_5.6_spmd.sunk | while | flops 101187584 | bytes 7128219 | solution.py:74
  112.8 2.7 dynamic_update_slice.21
  117.7 2.7 dynamic_update_slice.21
  122.7 2.7 dynamic_update_slice.21
  127.6 2.7 dynamic_update_slice.21
  132.6 2.7 dynamic_update_slice.21
  137.5 2.7 dynamic_update_slice.21
  142.5 2.7 dynamic_update_slice.21
  147.5 2.7 dynamic_update_slice.21
  152.4 2.7 dynamic_update_slice.21
  157.4 2.7 dynamic_update_slice.21
  182.1 2.7 dynamic_update_slice.21
  187.1 2.7 dynamic_update_slice.21
  192.0 2.7 dynamic_update_slice.21
  197.0 2.7 dynamic_update_slice.21
  201.9 2.7 dynamic_update_slice.21
  206.9 2.7 dynamic_update_slice.21
  211.8 2.7 dynamic_update_slice.21
  216.8 2.7 dynamic_update_slice.21
  276.0 107.2 %while.46 = (s32[]{:T(128)}, f32[32,192,128]{2,1,0:T(8,128)}, s32[32]{0:T(128)S(1)}, bf16[128,2079]{1,0:T(8,128)(2,1)S(1)}, bf16[128,2048]{1,0:T(8,128)(2,1)S(1)...) while((s32[]{:T(128)}, f32[32,192,128]{2,1,0:T(8,128)}, ...), condition=%wide.region_3.4_spmd, body=%wide.region_2.3_spmd.sunk | while | flops 100712448 | bytes 2130599 | solution.py:87
  386.4 37.2 %reduce-scatter.2.cloned.1.call-done = f32[8,192,128]{2,1,0:T(8,128)} async-done(((f32[32,192,128]{2,1,0:T(8,128)}), f32[8,192,128]{2,1,0:T(8,128)}) %reduce-scatter.2.cloned.1.call-update) | async-done | bytes 786448 | tf_op jit(solution)/shard_map/reduce_scatter | solution.py:86
  (310 shorter events, 271.6 us)
Async XLA Ops:
  7.2 14.2 %copy-start = (bf16[128,2048]{1,0:T(8,128)(2,1)S(1)}, bf16[128,2048]{1,0:T(8,128)(2,1)}, u32[]{:S(2)}) copy-start(bf16[128,2048]{1,0:T(8,128)(2,1)} %param.17) | copy-start | bytes 1572868
  7.2 21.8 %all-gather.2.cloned.1.call-start = ((), (), s32[]{:S(2)}) async-start(), calls=%async_computation.1 | async-start | bytes 1310720 | tf_op jit(solution)/shard_map/all_gather | solution.py:41
  7.9 375.4 %all-reduce.2.cloned.1.call-start = ((), (), s32[]{:S(2)}) async-start(), calls=%async_computation.3 | async-start | bytes 2097152 | tf_op jit(solution)/shard_map/psum | solution.py:105
  8.8 12.6 %collective-permute-start = (bf16[128,31]{1,0:T(8,128)(2,1)S(1)}, bf16[128,31]{1,0:T(8,128)(2,1)S(1)}, u32[]{:S(2)}, u32[]{:S(2)}) collective-permute-start(bf16[128,31]{1,0:T(8,128)(2,1)S(1)} %slice.35), channel_id=1, source_target_pairs={{0,1},{1,2},{2,3},{4,5},{5,6},{6,7},{8,9},{9,10},{10,11},{12,13},{... | collective-permute-start | bytes 23816 | tf_op jit(solution)/shard_map/ppermute | solution.py:14
  29.0 80.5 %copy-start.4 = (bf16[128,2048]{1,0:T(8,128)(2,1)S(1)}, bf16[128,2048]{1,0:T(8,128)(2,1)}, u32[]{:S(2)}) copy-start(bf16[128,2048]{1,0:T(8,128)(2,1)} %param.13) | copy-start | bytes 1572868
  109.5 1.0 copy-start.5
  268.6 3.5 collective-permute-start.1
  276.0 147.7 %reduce-scatter.2.cloned.1.call-start = ((), (), s32[]{:S(2)}) async-start(), calls=%async_computation.2 | async-start | bytes 3932160 | tf_op jit(solution)/shard_map/reduce_scatter | solution.py:86
  383.2 1.0 copy-start.1
  383.2 40.4 %copy-start.2 = (bf16[8,128,128]{2,1,0:T(8,128)(2,1)S(1)}, bf16[8,128,128]{2,1,0:T(8,128)(2,1)}, u32[]{:S(2)}) copy-start(bf16[8,128,128]{2,1,0:T(8,128)(2,1)} %param.15) | copy-start | bytes 786436
  383.2 42.3 %copy-start.3 = (bf16[8,64,128]{2,1,0:T(8,128)(2,1)S(1)}, bf16[8,64,128]{2,1,0:T(8,128)(2,1)}, u32[]{:S(2)}) copy-start(bf16[8,64,128]{2,1,0:T(8,128)(2,1)} %param.16) | copy-start | bytes 393220
Sparse Core Ops, SparseCore 0:
  9.6 19.4 all-gather.1
  276.1 80.4 all-reduce.1
  383.4 40.2 reduce-scatter.1
where the time goes:
time: 443 us; the launch traced here: 434 us
  matrix products  175 us (40%)
  local copies, waits for them, and re-layouts  110 us (25%)
  waiting for transfers between devices  47.2 us (11%)
  loops' own time  44.4 us (10%)
  other arithmetic  29.5 us (7%)
  between operations  13.9 us (3%)
  blocking collectives  10.2 us (2%)
    dynamic_update_slice x32, local copies, waits for them, and re-layouts, one_lag(): return lax.dynamic_update_slice_in_dim(acc, current + back, place, 1)  85.9 us
    dot_general x32, matrix products, one_lag(): jnp.dot(neuron_rows, win, preferred_element_type=jnp.float32)  43.7 us
    another operation x1, loops' own time, local(): lax.map(one_lag, jnp.arange(lags_here * lax.axis_size('tm'), dtype=jnp.in...  42 us
    reduce_scatter x1, waiting for transfers between devices, local(): lax.psum_scatter(lax.map(one_lag, jnp.arange(lags_here * lax.axis_size('t...  37.2 us
    dot_general x32, matrix products, one_lag(): jnp.dot(feature_rows, win, preferred_element_type=jnp.float32)  35.5 us
    dot_general x32, matrix products, one_lag(): lax.dot_general(feature_rows, resid_b, (((0,), (0,)), ((), ())), preferre...  35.4 us
    dot_general x32, matrix products, one_lag(): lax.dot_general(neuron_rows, resid_x, (((0,), (0,)), ((), ())), preferred...  34.9 us
    dynamic_update_slice x32, other arithmetic, local(): lax.map(one_lag, jnp.arange(lags_here * lax.axis_size('tm'), dtype=jnp.in...  20.9 us
  transfers between devices with their start and end apart: 5, of which 3 were waited for; matrix products, arithmetic and copies ran while one was open for 16% of the time, Pallas kernels for 0%

commit v1 on v0

v1 whole, which is shorter than its diff:
```python
import functools
import math

import jax
import jax.numpy as jnp
from jax import lax
from jax.experimental import pallas as pl
from jax.experimental.pallas import tpu as pltpu
from jax.sharding import PartitionSpec as P

behaviour_weight = 2.0
LANES = 128
MESH = pl.DeviceIdType.MESH
F32 = jnp.float32
BF16 = jnp.bfloat16


def remote(src, dst, send, recv, **where):
    return pltpu.make_async_remote_copy(
        src_ref=src, dst_ref=dst, send_sem=send, recv_sem=recv,
        device_id=where, device_id_type=MESH,
    )


def kernel(
    peers, direct, scale, rate_motif, rate_active, neurons, features, rows,
    data, beh, mot, bmot, act, o_mot, o_bmot, o_act,
    h_ext, ext, wst, wf, wt, acc, rext, r8, gbuf, gin, gown, gx, gx_in,
    halo_sem, w_send, w_recv, g_send, g_recv, *rest,
):
    lags = mot.shape[0]
    width, frames = act.shape
    groups = 4
    wide = lags * width
    me = lax.axis_index("tm")
    chip, core = me // 2, me % 2
    partner = 2 * chip + (1 - core)
    across = 2 * (1 - chip) + core
    diag = 2 * (1 - chip) + (1 - core)
    row = lax.axis_index("neuron")
    if direct:
        (hs, ph, ha1, hb1, ha2, hb2, sa, sb, pa, pb, y_send, y_recv, b1_send, b1_recv, a2_send,
         a2_recv, oaz_send, oaz_recv, oay_send, oay_recv, obz_send, obz_recv) = rest

    for j in range(lags):
        wst[me, j, :neurons, :] = mot[j]
        tail = bmot[j]
        if rows - neurons > features:
            tail = jnp.concatenate(
                [tail, jnp.zeros((rows - neurons - features, width), BF16)], axis=0)
        wst[me, j, neurons:, :] = tail

    barrier = pltpu.get_barrier_semaphore()
    for other in (partner, across, diag):
        pl.semaphore_signal(barrier, inc=1, device_id={"tm": other}, device_id_type=MESH)

    greeted = 3
    if direct:
        outer = peers // 2
        near = [row // 2 * 2 + 1 - row % 2]
        near += [(row // 2 + d) % outer * 2 + row % 2 for d in range(1, outer)]
        for other in near:
            pl.semaphore_signal(
                barrier, inc=1, device_id={"neuron": other}, device_id_type=MESH)
        greeted += len(near)
    pl.semaphore_wait(barrier, greeted)

    act_halo = remote(act.at[:, frames - LANES:], ext.at[:, :LANES],
                      halo_sem.at[0], halo_sem.at[1], tm=(me + 1) % groups)
    pl.when(me < groups - 1)(act_halo.start)
    w_across = remote(wst.at[me], wst.at[me], w_send.at[0], w_recv.at[0], tm=across)
    w_across.start()
    w_partner = remote(wst.at[me], wst.at[me], w_send.at[1], w_recv.at[1], tm=partner)
    w_partner.start()
    w_relay = remote(wst.at[across], wst.at[across], w_send.at[2], w_recv.at[2], tm=partner)

    ext[:, LANES:] = act[...]

    @pl.when(me == 0)
    def _():
        ext[:, :LANES] = jnp.zeros((width, LANES), BF16)

    pl.when(me > 0)(act_halo.wait_recv)

    def spread(b, c):
        at = pl.multiple_of(b * 16, 16)
        x = ext[pl.ds(at, 16), :]
        for lag in range(groups * lags):
            y = x if lag == 0 else pltpu.roll(x, lag, 1)
            h_ext[pl.ds(lag * width + at, 16), :] = y[:, LANES:]
        return c

    lax.fori_loop(0, width // 16, spread, 0)

    step = 512

    def side(g):
        for j in range(lags):
            wf[:, j * width:(j + 1) * width] = wst[g, j]
        wt[pl.ds(pl.multiple_of(g * width, width), width), :] = (
            wst[g].reshape(lags * rows, width).T)

    def forward(g, first, last):
        side(g)
        base = pl.multiple_of(g * wide, wide)

        def body(c, carry):
            cols = pl.ds(pl.multiple_of(c * step, step), step)
            v = jnp.dot(wf[...], h_ext[pl.ds(base, wide), cols], preferred_element_type=F32)
            if not first:
                v = acc[:, cols] + v
            if not last:
                acc[:, cols] = v
                return carry
            rext[:neurons, cols] = (
                data[:, cols].astype(F32) - scale * v[:neurons]).astype(BF16)
            tail = (behaviour_weight * (
                beh[:, cols].astype(F32) - scale * v[neurons:neurons + features])).astype(BF16)
            if rows - neurons > features:
                tail = jnp.concatenate(
                    [tail, jnp.zeros((rows - neurons - features, step), BF16)], axis=0)
            rext[neurons:, cols] = tail
            return carry

        if not last:
            lax.fori_loop(0, frames // step, body, 0)
            return
        body(0, 0)
        pl.when(me > 0)(r_halo.start)
        lax.fori_loop(1, frames // step, body, 0)

    r_halo = remote(rext.at[:, :LANES], rext.at[:, frames:],
                    halo_sem.at[2], halo_sem.at[3], tm=(me + groups - 1) % groups)
    forward(me, True, False)
    w_partner.wait_recv()
    forward(partner, False, False)
    w_across.wait_recv()
    w_relay.start()
    forward(across, False, False)
    w_relay.wait_recv()
    forward(diag, False, True)

    @pl.when(me == groups - 1)
    def _():
        rext[:, frames:] = jnp.zeros((rows, LANES), BF16)

    pl.when(me < groups - 1)(r_halo.wait_recv)

    def spread_back(b, c):
        at = pl.multiple_of(b * 16, 16)
        x = rext[pl.ds(at, 16), :]
        for j in range(lags):
            y = x if j == 0 else pltpu.roll(x, frames + LANES - j, 1)
            r8[pl.ds(j * rows + at, 16), :] = y
        return c

    lax.fori_loop(0, rows // 16, spread_back, 0)

    def back(c):
        at = pl.multiple_of(c * step, step)
        v = jnp.dot(wt[...], r8[:, pl.ds(at, step + LANES)], preferred_element_type=F32)
        total = v[:width, :step]
        for g in range(1, groups):
            total = total + v[g * width:(g + 1) * width, g * lags:g * lags + step]
        if not direct:
            o_act[:, pl.ds(at, step)] = total
            return
        ph[:, pl.ds(at, step)] = total
        mean, rest = centred(total)
        hs[:width, pl.ds(at, step)] = rest
        hs[width:, pl.ds(at, step)] = mean

    def centred(total):
        mean = jnp.mean(total, axis=0, keepdims=True).astype(BF16)
        rest = (total - mean.astype(F32)).astype(BF16)
        return jnp.broadcast_to(mean, (16, total.shape[1])), rest

    def whole(part):
        return part[:width].astype(F32) + part[width:width + 1].astype(F32)

    def fresh(at, total):
        lanes = pl.ds(at, LANES)
        o_act[:, lanes] = jnp.maximum(
            act[:, lanes].astype(F32) + (rate_active * scale) * total, 0.0).astype(BF16)

    if not direct:
        for c in range(frames // step):
            back(c)
    else:
        half = frames // 2
        quarter = frames // 4
        outer = peers // 2
        inner, far = row % 2, row // 2
        beside = far * 2 + (1 - inner)
        others = [(far + d) % outer for d in range(1, outer)]
        pair = half // outer

        def lanes_at(at, size):
            return pl.ds(pl.multiple_of(at, LANES), size)

        def first_b(to, sender):
            return remote(hs.at[:, lanes_at(half + to * pair, pair)], hb1.at[sender],
                          b1_send.at[to], b1_recv.at[sender], neuron=to * 2 + inner)

        a1 = remote(hs.at[:, lanes_at((1 - inner) * quarter, quarter)], ha1,
                    y_send.at[0], y_recv.at[0], neuron=beside)

        back(2)
        back(3)
        for z in others:
            first_b(z, far).start()
        back(1 - inner)
        a1.start()
        back(inner)

        def second_a(to, sender):
            return remote(sa.at[:, lanes_at(to * LANES, LANES)], ha2.at[sender],
                          a2_send.at[to], a2_recv.at[sender], neuron=to * 2 + inner)

        b2 = remote(sb.at[:, lanes_at((1 - inner) * LANES, LANES)], hb2,
                    y_send.at[1], y_recv.at[1], neuron=beside)

        def stage_two():
            a1.wait_recv()
            total = ph[:, lanes_at(inner * quarter, quarter)] + whole(ha1[...])
            pa[...] = total
            sa[width:], sa[:width] = centred(total)
            for z in others:
                second_a(z, far).start()
            total = ph[:, lanes_at(half + far * pair, pair)]
            for z in others:
                first_b(far, z).wait_recv()
                total = total + whole(hb1[z])
            pb[...] = total
            sb[width:], sb[:width] = centred(total)
            b2.start()

        def place_a(z, y):
            return pl.multiple_of(y * quarter + z * LANES, LANES)

        def place_b(z, y):
            return pl.multiple_of(half + z * pair + y * LANES, LANES)

        def out_copy(at, send, recv, to):
            piece = o_act.at[:, pl.ds(at, LANES)]
            return remote(piece, piece, send, recv, neuron=to)

        def az(to, owner):
            return out_copy(place_a(owner, inner), oaz_send.at[to], oaz_recv.at[owner],
                            to * 2 + inner)

        def ay(z, y):
            return out_copy(place_a(z, y), oay_send.at[z], oay_recv.at[z], beside)

        def by(y):
            return out_copy(place_b(far, y), y_send.at[2], y_recv.at[2], beside)

        def bz(to, owner, y, slot):
            return out_copy(place_b(owner, y), obz_send.at[slot, to], obz_recv.at[slot, owner],
                            to * 2 + inner)

        def stage_three():
            total = pa[:, lanes_at(far * LANES, LANES)]
            for z in others:
                second_a(far, z).wait_recv()
                total = total + whole(ha2[z])
            fresh(place_a(far, inner), total)
            for z in others:
                az(z, far).start()
            ay(far, inner).start()
            b2.wait_recv()
            fresh(place_b(far, inner), pb[:, lanes_at(inner * LANES, LANES)] + whole(hb2[...]))
            by(inner).start()
            for z in others:
                bz(z, far, inner, 0).start()

        def stage_four():
            by(1 - inner).wait_recv()
            for z in others:
                bz(z, far, 1 - inner, 1).start()
            for z in others:
                az(far, z).wait_recv()
                ay(z, inner).start()

        def stage_five():
            for z in others:
                bz(far, z, inner, 0).wait_recv()
                bz(far, z, 1 - inner, 1).wait_recv()
            for z in range(outer):
                ay(z, 1 - inner).wait_recv()
                ay(z, inner).wait_send()
            for z in others:
                first_b(z, far).wait_send()
                second_a(z, far).wait_send()
                az(z, far).wait_send()
                bz(z, far, inner, 0).wait_send()
                bz(z, far, 1 - inner, 1).wait_send()
            a1.wait_send()
            b2.wait_send()
            by(inner).wait_send()

    def grad(g, buffer):
        base = pl.multiple_of(g * wide, wide)

        def body(c, carry):
            at = pl.multiple_of(c * 256, 256)
            buffer[:, pl.ds(at, 256)] = lax.dot_general(
                rext[:, :frames], h_ext[pl.ds(base + at, 256), :],
                (((1,), (1,)), ((), ())), preferred_element_type=F32)
            return carry

        lax.fori_loop(0, wide // 256, body, 0)

    grad(diag, gbuf.at[0])
    g_diag = remote(gbuf.at[0], gin.at[0], g_send.at[0], g_recv.at[0], tm=partner)
    g_diag.start()
    if direct:
        stage_two()
    grad(across, gown)
    g_diag.wait_recv()
    total = gown[...] + gin[0]
    mean = jnp.mean(total, axis=1, keepdims=True).astype(BF16)
    gx[:, :wide] = (total - mean.astype(F32)).astype(BF16)
    gx[:, wide:] = jnp.broadcast_to(mean, (rows, LANES))
    g_across = remote(gx, gx_in, g_send.at[1], g_recv.at[1], tm=across)
    g_across.start()
    if direct:
        stage_three()
    grad(partner, gbuf.at[1])
    g_partner = remote(gbuf.at[1], gin.at[1], g_send.at[2], g_recv.at[2], tm=partner)
    g_partner.start()
    if direct:
        stage_four()
    grad(me, gown)
    g_partner.wait_recv()
    g_across.wait_recv()
    back_mean = gx_in[:, wide:].astype(F32)
    for j in range(lags):
        cols = slice(j * width, (j + 1) * width)
        g = gown[:, cols] + gin[1, :, cols] + (gx_in[:, cols].astype(F32) + back_mean)
        g = (rate_motif * scale) * g
        o_mot[j] = jnp.maximum(mot[j].astype(F32) + g[:neurons], 0.0).astype(BF16)
        o_bmot[j] = jnp.maximum(
            bmot[j].astype(F32) + g[neurons:neurons + features], 0.0).astype(BF16)
    if direct:
        stage_five()
    pl.when(me < groups - 1)(act_halo.wait_send)
    pl.when(me > 0)(r_halo.wait_send)
    for copy in (w_across, w_partner, w_relay, g_diag, g_across, g_partner):
        copy.wait_send()


def local(peers, groups, data, behaviour, motifs, behav_motifs, activations):
    lags, neurons, width = motifs.shape
    features = behaviour.shape[0]
    frames = activations.shape[1]
    lag_count = lags * groups
    scale = 1.0 / (lag_count * width)
    rate_motif = 0.5 * lag_count * width / math.sqrt(frames * groups)
    rate_active = 0.5 * lag_count * width / math.sqrt(
        lag_count * (neurons * peers + 4 * features * peers))
    rows = neurons + -(-features // 16) * 16
    wide = lags * width
    direct = frames // (2 * peers) == LANES and peers % 2 == 0
    outer = max(peers // 2, 1)
    dma = pltpu.SemaphoreType.DMA
    vmem = pl.BlockSpec(memory_space=pltpu.VMEM)
    flops = 6 * rows * lag_count * width * frames
    scratch = [
        pltpu.VMEM((lag_count * width, frames), BF16),
        pltpu.VMEM((width, frames + LANES), BF16),
        pltpu.VMEM((groups, lags, rows, width), BF16),
        pltpu.VMEM((rows, wide), BF16),
        pltpu.VMEM((groups * width, lags * rows), BF16),
        pltpu.VMEM((rows, frames), F32),
        pltpu.VMEM((rows, frames + LANES), BF16),
        pltpu.VMEM((lags * rows, frames + LANES), BF16),
        pltpu.VMEM((2, rows, wide), F32),
        pltpu.VMEM((2, rows, wide), F32),
        pltpu.VMEM((rows, wide), F32),
        pltpu.VMEM((rows, wide + LANES), BF16),
        pltpu.VMEM((rows, wide + LANES), BF16),
        dma((4,)), dma((3,)), dma((3,)), dma((3,)), dma((3,)),
    ]
    if direct:
        tall, quarter, pair = width + 16, frames // 4, frames // 2 // outer
        scratch += [
            pltpu.VMEM((tall, frames), BF16),
            pltpu.VMEM((width, frames), F32),
            pltpu.VMEM((tall, quarter), BF16),
            pltpu.VMEM((outer, tall, pair), BF16),
            pltpu.VMEM((outer, tall, LANES), BF16),
            pltpu.VMEM((tall, LANES), BF16),
            pltpu.VMEM((tall, quarter), BF16),
            pltpu.VMEM((tall, pair), BF16),
            pltpu.VMEM((width, quarter), F32),
            pltpu.VMEM((width, pair), F32),
            dma((3,)), dma((3,)),
            dma((outer,)), dma((outer,)), dma((outer,)), dma((outer,)),
            dma((outer,)), dma((outer,)), dma((outer,)), dma((outer,)),
            dma((2, outer)), dma((2, outer)),
        ]
    out = pl.pallas_call(
        functools.partial(kernel, peers, direct, scale, rate_motif, rate_active,
                          neurons, features, rows),
        out_shape=(
            jax.ShapeDtypeStruct(motifs.shape, BF16),
            jax.ShapeDtypeStruct(behav_motifs.shape, BF16),
            jax.ShapeDtypeStruct(activations.shape, BF16 if direct else F32),
        ),
        in_specs=[vmem] * 5,
        out_specs=[vmem] * 3,
        scratch_shapes=scratch,
        compiler_params=pltpu.CompilerParams(
            collective_id=0, has_side_effects=True, vmem_limit_bytes=60 * 1024 * 1024),
        cost_estimate=pl.CostEstimate(
            flops=flops, bytes_accessed=4 * 1024 * 1024, transcendentals=0),
    )(data, behaviour, motifs, behav_motifs, activations)
    if direct:
        return out
    grad = (rate_active * scale) * lax.psum(out[2], "neuron")
    return out[0], out[1], jnp.maximum(activations.astype(F32) + grad, 0.0).astype(BF16)


def solution(mesh):
    placed = (
        P("neuron", "tm"),
        P("neuron", "tm"),
        P("tm", "neuron", None),
        P("tm", "neuron", None),
        P(None, "tm"),
    )
    return jax.shard_map(
        functools.partial(local, mesh.shape["neuron"], mesh.shape["tm"]),
        mesh=mesh,
        in_specs=placed,
        out_specs=(P("tm", "neuron", None), P("tm", "neuron", None), P(None, "tm")),
        check_vma=False,
    )
```

time: 443 us -> 54.2 us (0.12); the launches traced: 434 us -> 54 us
  matrix products: 175 us -> 0 us
  local copies, waits for them, and re-layouts: 110 us -> 4.09 us
  Pallas kernels: 0 us -> 49.3 us
  waiting for transfers between devices: 47.2 us -> 0 us
  loops' own time: 44.4 us -> 0 us
  other arithmetic: 29.5 us -> 0 us
  between operations: 13.9 us -> 0.65 us
  blocking collectives: 10.2 us -> 0 us
    dot_general x192 -> x0, matrix products: 175 us -> none  [the longest x32 43.7 us: one_lag(): jnp.dot(neuron_rows, win, preferred_element_type=jnp.float32)]
    dynamic_update_slice x32 -> x0, local copies, waits for them, and re-layouts: 85.9 us -> none  [one_lag(): return lax.dynamic_update_slice_in_dim(acc, current + back, place, 1)]
    pallas_call x0 -> x1, Pallas kernels: none -> 49.3 us  [local(): pl.pallas_call(functools.partial(kernel, peers, direct, scale, rate_motif...]
    another operation x3 -> x0, loops' own time: 44.4 us -> none  [the longest x1 42 us: local(): lax.map(one_lag, jnp.arange(lags_here * lax.axis_size('tm'), dtype=jnp.in...]
    reduce_scatter x1 -> x0, waiting for transfers between devices: 37.2 us -> none  [local(): lax.psum_scatter(lax.map(one_lag, jnp.arange(lags_here * lax.axis_size('t...]
    dynamic_update_slice x32 -> x0, other arithmetic: 20.9 us -> none  [local(): lax.map(one_lag, jnp.arange(lags_here * lax.axis_size('tm'), dtype=jnp.in...]
    dynamic_slice x32 -> x0, local copies, waits for them, and re-layouts: 18.6 us -> none  [local(): lax.map(one_lag, jnp.arange(lags_here * lax.axis_size('tm'), dtype=jnp.in...]
    all_gather x1 -> x0, blocking collectives: 10.2 us -> none  [local(): lax.all_gather(behav_motifs, 'tm', axis=0, tiled=True)]
  transfers between devices with their start and end apart: 5 -> 0, of which waited for: 3 -> 0; matrix products, arithmetic and copies ran while one was open for 16% -> 0% of each run, Pallas kernels for 0% -> 0%
where the time goes in v1:
time: 54.2 us; the launch traced here: 54 us
  Pallas kernels  49.3 us (91%)
  local copies, waits for them, and re-layouts  4.09 us (8%)
  between operations  0.65 us (1%)
    pallas_call x1, Pallas kernels, local(): pl.pallas_call(functools.partial(kernel, peers, direct, scale, rate_motif...  49.3 us
    unnamed x5, local copies, waits for them, and re-layouts  4.09 us

profile of v1, /device:TPU:0, one launch (start us, length us, event | category | flops | bytes accessed | tf_op | source)
XLA Modules:
  0.0 54.0 jit_solution(13323997671071527030)
XLA Ops:
  0.6 49.3 %shard_map.76 = (bf16[8,128,128]{2,1,0:T(8,128)(2,1)}, bf16[8,64,128]{2,1,0:T(8,128)(2,1)}, bf16[128,2048]{1,0:T(8,128)(2,1)}) custom-call(bf16[128,2048]{1,0:T(8,128)(2,1)} %data.1, bf16[64,2048]{1,0:T(8,128)(2,1)} %beh.1, bf16[8,128,128]{2,1,0:T(8,128)(2,1)} %mot.1, bf16[8,64,128]{2,1,0:T(8,128)(2,1)} %bmot.1, bf16[128,2048]{1,0:T(8,128)(2,1)} %act.1), custom_call_target="tpu_custom_call" | custom-call | flops 9663676416 | bytes 4194304 | tf_op jit(solution)/shard_map/pallas_call | solution.py:403
  49.9 0.0 copy-start
  49.9 1.7 %copy.11 = bf16[8,128,128]{2,1,0:T(8,128)(2,1)} copy(bf16[8,128,128]{2,1,0:T(8,128)(2,1)} %get-tuple-element.6) | data formatting | bytes 524288
  51.6 1.6 %copy.12 = bf16[8,64,128]{2,1,0:T(8,128)(2,1)} copy(bf16[8,64,128]{2,1,0:T(8,128)(2,1)} %get-tuple-element.7) | data formatting | bytes 262144
  53.2 0.0 copy-done
  53.2 0.8 %copy.13 = bf16[128,2048]{1,0:T(8,128)(2,1)} copy(bf16[128,2048]{1,0:T(8,128)(2,1)S(1)} %copy-done) | data formatting | bytes 1048576
Async XLA Ops:
  49.9 3.3 %copy-start = (bf16[128,2048]{1,0:T(8,128)(2,1)S(1)}, bf16[128,2048]{1,0:T(8,128)(2,1)}, u32[]{:S(2)}) copy-start(bf16[128,2048]{1,0:T(8,128)(2,1)} %get-tuple-element.8) | copy-start | bytes 1572868

commit v2 on v1

--- a/solution.py
+++ b/solution.py
@@ -92,7 +92,7 @@
 
     lax.fori_loop(0, width // 16, spread, 0)
 
-    step = 512
+    step = frames // 2
 
     def side(g):
         for j in range(lags):
@@ -104,30 +104,29 @@
         side(g)
         base = pl.multiple_of(g * wide, wide)
 
-        def body(c, carry):
-            cols = pl.ds(pl.multiple_of(c * step, step), step)
+        def body(at, size):
+            cols = slice(at, at + size)
             v = jnp.dot(wf[...], h_ext[pl.ds(base, wide), cols], preferred_element_type=F32)
             if not first:
                 v = acc[:, cols] + v
             if not last:
                 acc[:, cols] = v
-                return carry
+                return
             rext[:neurons, cols] = (
                 data[:, cols].astype(F32) - scale * v[:neurons]).astype(BF16)
             tail = (behaviour_weight * (
                 beh[:, cols].astype(F32) - scale * v[neurons:neurons + features])).astype(BF16)
             if rows - neurons > features:
                 tail = jnp.concatenate(
-                    [tail, jnp.zeros((rows - neurons - features, step), BF16)], axis=0)
+                    [tail, jnp.zeros((rows - neurons - features, size), BF16)], axis=0)
             rext[neurons:, cols] = tail
-            return carry
 
         if not last:
-            lax.fori_loop(0, frames // step, body, 0)
+            body(0, frames)
             return
-        body(0, 0)
+        body(0, step)
         pl.when(me > 0)(r_halo.start)
-        lax.fori_loop(1, frames // step, body, 0)
+        body(step, frames - step)
 
     r_halo = remote(rext.at[:, :LANES], rext.at[:, frames:],
                     halo_sem.at[2], halo_sem.at[3], tm=(me + groups - 1) % groups)
@@ -157,7 +156,7 @@
     lax.fori_loop(0, rows // 16, spread_back, 0)
 
     def back(c):
-        at = pl.multiple_of(c * step, step)
+        at = c * step
         v = jnp.dot(wt[...], r8[:, pl.ds(at, step + LANES)], preferred_element_type=F32)
         total = v[:width, :step]
         for g in range(1, groups):
@@ -205,13 +204,11 @@
         a1 = remote(hs.at[:, lanes_at((1 - inner) * quarter, quarter)], ha1,
                     y_send.at[0], y_recv.at[0], neuron=beside)
 
-        back(2)
-        back(3)
+        back(1)
         for z in others:
             first_b(z, far).start()
-        back(1 - inner)
+        back(0)
         a1.start()
-        back(inner)
 
         def second_a(to, sender):
             return remote(sa.at[:, lanes_at(to * LANES, LANES)], ha2.at[sender],
@@ -301,15 +298,9 @@
 
     def grad(g, buffer):
         base = pl.multiple_of(g * wide, wide)
-
-        def body(c, carry):
-            at = pl.multiple_of(c * 256, 256)
-            buffer[:, pl.ds(at, 256)] = lax.dot_general(
-                rext[:, :frames], h_ext[pl.ds(base + at, 256), :],
-                (((1,), (1,)), ((), ())), preferred_element_type=F32)
-            return carry
-
-        lax.fori_loop(0, wide // 256, body, 0)
+        buffer[...] = lax.dot_general(
+            rext[:, :frames], h_ext[pl.ds(base, wide), :],
+            (((1,), (1,)), ((), ())), preferred_element_type=F32)
 
     grad(diag, gbuf.at[0])
     g_diag = remote(gbuf.at[0], gin.at[0], g_send.at[0], g_recv.at[0], tm=partner)
@@ -348,6 +339,15 @@
     pl.when(me > 0)(r_halo.wait_send)
     for copy in (w_across, w_partner, w_relay, g_diag, g_across, g_partner):
         copy.wait_send()
+
+
+def hand_over(a, b, c, x, y, z, sem):
+    copies = [pltpu.make_async_copy(src, dst, sem.at[i])
+              for i, (src, dst) in enumerate(((a, x), (b, y), (c, z)))]
+    for copy in copies:
+        copy.start()
+    for copy in copies:
+        copy.wait()
 
 
 def local(peers, groups, data, behaviour, motifs, behav_motifs, activations):
@@ -417,7 +417,13 @@
             flops=flops, bytes_accessed=4 * 1024 * 1024, transcendentals=0),
     )(data, behaviour, motifs, behav_motifs, activations)
     if direct:
-        return out
+        return pl.pallas_call(
+            hand_over,
+            out_shape=tuple(jax.ShapeDtypeStruct(o.shape, o.dtype) for o in out),
+            in_specs=[pl.BlockSpec(memory_space=pl.ANY)] * 3,
+            out_specs=[pl.BlockSpec(memory_space=pl.ANY)] * 3,
+            scratch_shapes=[dma((3,))],
+        )(*out)
     grad = (rate_active * scale) * lax.psum(out[2], "neuron")
     return out[0], out[1], jnp.maximum(activations.astype(F32) + grad, 0.0).astype(BF16)
 

time: 54.2 us -> 79.4 us (1.46)
  Pallas kernels: 49.3 us -> 78.5 us
  local copies, waits for them, and re-layouts: 4.09 us -> 0 us
    pallas_call x0 -> x1, Pallas kernels: none -> 28.9 us  [local(): pl.pallas_call(hand_over, out_shape=tuple((jax.ShapeDtypeStruct(o.shape,...]
    unnamed x5 -> x0, local copies, waits for them, and re-layouts: 4.09 us -> none
where the time goes in v2:
time: 79.4 us; the launch traced here: 79.3 us
  Pallas kernels  78.5 us (99%)
  between operations  0.8 us (1%)
    pallas_call x1, Pallas kernels, local(): pl.pallas_call(functools.partial(kernel, peers, direct, scale, rate_motif...  49.5 us
    pallas_call x1, Pallas kernels, local(): pl.pallas_call(hand_over, out_shape=tuple((jax.ShapeDtypeStruct(o.shape,...  28.9 us

profile of v2, /device:TPU:0, one launch (start us, length us, event | category | flops | bytes accessed | tf_op | source)
XLA Modules:
  0.0 79.3 jit_solution(13734837829500061237)
XLA Ops:
  0.6 49.5 %shard_map.76 = (bf16[8,128,128]{2,1,0:T(8,128)(2,1)}, bf16[8,64,128]{2,1,0:T(8,128)(2,1)}, bf16[128,2048]{1,0:T(8,128)(2,1)}) custom-call(bf16[128,2048]{1,0:T(8,128)(2,1)} %data.1, bf16[64,2048]{1,0:T(8,128)(2,1)} %beh.1, bf16[8,128,128]{2,1,0:T(8,128)(2,1)} %mot.1, bf16[8,64,128]{2,1,0:T(8,128)(2,1)} %bmot.1, bf16[128,2048]{1,0:T(8,128)(2,1)} %act.1), custom_call_target="tpu_custom_call" | custom-call | flops 9663676416 | bytes 4194304 | tf_op jit(solution)/shard_map/pallas_call | solution.py:403
  50.2 28.9 %shard_map.77 = (bf16[8,128,128]{2,1,0:T(8,128)(2,1)}, bf16[8,64,128]{2,1,0:T(8,128)(2,1)}, bf16[128,2048]{1,0:T(8,128)(2,1)}) custom-call(bf16[8,128,128]{2,1,0:T(8,128)(2,1)} %get-tuple-element.6.a, bf16[8,64,128]{2,1,0:T(8,128)(2,1)} %get-tuple-element.7.b, bf16[128,2048]{1,0:T(8,128)(2,1)} %get-tuple-element.8.c), custom_call_target="tpu_custom_call" | custom-call | tf_op jit(solution)/shard_map/pallas_call | solution.py:420
